TPU v7x, 32 devices: a whole 2x2x4 slice. The times are simulated.
32 devices in a mesh: dp: 8 (over z, x), head: 4 (over y, core).
Axes of the slice: x: 2, y: 2, z: 4, core: 2. Of those that a mesh axis runs over, the one named last changes fastest.
Arguments:
- tokens: bfloat16 [32768, 768], P(('dp', 'head')), may hold values from -6 to 6
- cotangent: bfloat16 [32768, 768], P(('dp', 'head')), may hold values from -6 to 6
- w_qkv: bfloat16 [768, 12, 192], P(None, 'head'), may hold values from -0.21875 to 0.21875
- bias_qv: bfloat16 [12, 2, 64], P('head'), may hold values from -3 to 3
- w_out: bfloat16 [12, 64, 768], P('head'), may hold values from -1.25 to 1.25
- bias_out: float32 [768], replicated, may hold values from -3 to 3
- gain_one: float32 [768], replicated, may hold values from 0.5 to 1.5
- beta_one: float32 [768], replicated, may hold values from -3 to 3
- w_up: bfloat16 [768, 3072], replicated, may hold values from -0.21875 to 0.21875
- bias_up: float32 [3072], replicated, may hold values from -3 to 3
- w_down: bfloat16 [3072, 768], replicated, may hold values from -0.109375 to 0.109375
- bias_down: float32 [768], replicated, may hold values from -3 to 3
- gain_two: float32 [768], replicated, may hold values from 0.5 to 1.5
- beta_two: float32 [768], replicated, may hold values from -3 to 3
Outputs:
- layer_out: bfloat16 [32768, 768], P(('dp', 'head'))
- input_grad: float32 [32768, 768], P(('dp', 'head'))
- grad_qkv: float32 [768, 12, 192], P('dp', 'head')
- grad_bias_qv: float32 [12, 2, 64], P('head', None, 'dp')
- grad_out: float32 [12, 64, 768], P('head', None, 'dp')
- grad_bias_out: float32 [768], replicated
- grad_gain_one: float32 [768], replicated
- grad_beta_one: float32 [768], replicated
- grad_w_up: float32 [768, 3072], replicated
- grad_bias_up: float32 [3072], replicated
- grad_w_down: float32 [3072, 768], replicated
- grad_bias_down: float32 [768], replicated
- grad_gain_two: float32 [768], replicated
- grad_beta_two: float32 [768], replicated
All inputs are finite; a program needn't handle non-finite values.
Results may differ from a plain program's by a relative error of at most 0.017.
Values may be sent and summed in bfloat16 or wider, within the bound.
No kernel may reach another device: no remote copies, remote signals or barrier semaphores. Data moves between devices by JAX's collectives and lax.ppermute only.
A program may use at most 192 MiB of HBM per device.

v0:
```python
import math

import jax
import jax.numpy as jnp
from jax import lax
from jax.sharding import PartitionSpec as P

SEQ = 128


epsilon = 1e-12


def matmul_rows(left, right):
    return lax.dot_general(
        left, right, (((0,), (0,)), ((), ())), preferred_element_type=jnp.float32
    )


def matmul_back(left, right):
    return lax.dot_general(
        left, right, (((1,), (1,)), ((), ())), preferred_element_type=jnp.float32
    )


def gelu_exact(values):
    return jax.nn.gelu(values, approximate=False)


def normalize(values, norm_gain, norm_shift):
    center = values - jnp.mean(values, axis=-1, keepdims=True)
    variance = jnp.mean(center * center, axis=-1, keepdims=True)
    inverse = lax.rsqrt(variance + epsilon)
    normal_rows = center * inverse
    return (normal_rows * norm_gain + norm_shift, normal_rows, inverse)


def normalize_back(upstream, normal_rows, inverse, norm_gain):
    grad_unit = upstream * norm_gain
    grad_rows = inverse * (
        grad_unit
        - jnp.mean(grad_unit, axis=-1, keepdims=True)
        - normal_rows * jnp.mean(grad_unit * normal_rows, axis=-1, keepdims=True)
    )
    return (grad_rows, jnp.sum(upstream * normal_rows, axis=0), jnp.sum(upstream, axis=0))


def split_blocks(projected, head_count, seq_length):
    sequences = projected.shape[0] // seq_length
    per_block = math.gcd(sequences, max(1, 512 // seq_length))
    return projected.reshape(sequences // per_block, per_block, seq_length, head_count, 3, -1)


def score_block(queries, keyed):
    factor = float(queries.shape[-1]) ** (-0.5)
    return (
        jnp.einsum("bqhd,bkhd->bhqk", queries, keyed, preferred_element_type=jnp.float32) * factor
    )


def attend_block(section):
    queries = section[:, :, :, 0]
    keyed = section[:, :, :, 1]
    valued = section[:, :, :, 2]
    scores = score_block(queries, keyed)
    highest = jnp.max(scores, axis=-1, keepdims=True)
    exponent = jnp.exp(scores - highest)
    row_total = jnp.sum(exponent, axis=-1, keepdims=True)
    attn_probs = exponent / row_total
    context = jnp.einsum(
        "bhqk,bkhd->bqhd",
        attn_probs.astype(jnp.bfloat16),
        valued,
        preferred_element_type=jnp.float32,
    )
    return (context.astype(jnp.bfloat16), highest + jnp.log(row_total))


def attend_back(pieces):
    section, log_total, grad_context = pieces
    queries = section[:, :, :, 0]
    keyed = section[:, :, :, 1]
    valued = section[:, :, :, 2]
    factor = float(queries.shape[-1]) ** (-0.5)
    attn_probs = jnp.exp(score_block(queries, keyed) - log_total)
    grad_probs = jnp.einsum(
        "bqhd,bkhd->bhqk", grad_context, valued, preferred_element_type=jnp.float32
    )
    inner = jnp.sum(grad_probs * attn_probs, axis=-1, keepdims=True)
    grad_scores = (attn_probs * (grad_probs - inner)).astype(jnp.bfloat16)
    grad_values = jnp.einsum(
        "bhqk,bqhd->bkhd",
        attn_probs.astype(jnp.bfloat16),
        grad_context,
        preferred_element_type=jnp.float32,
    )
    grad_queries = (
        jnp.einsum("bhqk,bkhd->bqhd", grad_scores, keyed, preferred_element_type=jnp.float32)
        * factor
    )
    grad_keyed = (
        jnp.einsum("bhqk,bqhd->bkhd", grad_scores, queries, preferred_element_type=jnp.float32)
        * factor
    )
    return jnp.stack([grad_queries, grad_keyed, grad_values], axis=-2).astype(jnp.bfloat16)


def attention_forward(projected, head_count, seq_length):
    sections = split_blocks(projected, head_count, seq_length)
    context, log_total = lax.map(attend_block, sections)
    return (context.reshape(projected.shape[0], -1), log_total)


def attention_backward(projected, log_total, grad_context, head_count, seq_length):
    sections = split_blocks(projected, head_count, seq_length)
    grad_shaped = grad_context.reshape(sections.shape[:4] + (-1,))
    grads = lax.map(attend_back, (sections, log_total, grad_shaped))
    return grads.reshape(projected.shape[0], -1)


def project(inputs, weight, bias_pair):
    model_width = weight.shape[0]
    raw_qkv = jnp.dot(inputs, weight.reshape(model_width, -1), preferred_element_type=jnp.float32)
    bias_wide = bias_pair.astype(jnp.float32)
    full_bias = jnp.stack(
        [bias_wide[:, 0], jnp.zeros_like(bias_wide[:, 0]), bias_wide[:, 1]], axis=1
    )
    return (raw_qkv + full_bias.reshape(-1)).astype(jnp.bfloat16)


def pair_sums(grad_projected, head_count):
    column_sums = jnp.sum(grad_projected, axis=0, dtype=jnp.float32).reshape(head_count, 3, -1)
    return jnp.stack([column_sums[:, 0], column_sums[:, 2]], axis=1)


def shards(
    tokens,
    cotangent,
    w_qkv,
    bias_qv,
    w_out,
    bias_out,
    gain_one,
    beta_one,
    w_up,
    bias_up,
    w_down,
    bias_down,
    gain_two,
    beta_two,
):
    model_width = tokens.shape[1]
    local_heads = w_qkv.shape[1]
    gathered = lax.all_gather(tokens, "head", axis=0, tiled=True)
    projected = project(gathered, w_qkv, bias_qv)
    context, log_total = attention_forward(projected, local_heads, SEQ)
    out_rows = w_out.reshape(-1, model_width)
    picked = context
    attention = (
        lax.psum_scatter(
            jnp.dot(picked, out_rows, preferred_element_type=jnp.float32).astype(jnp.bfloat16),
            "head",
            scatter_dimension=0,
            tiled=True,
        ).astype(jnp.float32)
        + bias_out
    )
    normed_one, unit_one, scale_one = normalize(
        tokens.astype(jnp.float32) + attention, gain_one, beta_one
    )
    normed_low = normed_one.astype(jnp.bfloat16)
    hidden_pre = jnp.dot(normed_low, w_up, preferred_element_type=jnp.float32) + bias_up
    gelu_value, gelu_pull = jax.vjp(gelu_exact, hidden_pre)
    activated = gelu_value.astype(jnp.bfloat16)
    ffn_out = jnp.dot(activated, w_down, preferred_element_type=jnp.float32) + bias_down
    result, unit_two, scale_two = normalize(normed_one + ffn_out, gain_two, beta_two)
    layer_out = result.astype(jnp.bfloat16)
    upstream = cotangent.astype(jnp.float32)
    grad_two, grad_gain_two, grad_beta_two = normalize_back(upstream, unit_two, scale_two, gain_two)
    grad_ffn = grad_two.astype(jnp.bfloat16)
    grad_bias_down = jnp.sum(grad_ffn, axis=0, dtype=jnp.float32)
    grad_w_down = matmul_rows(activated, grad_ffn)
    grad_active = matmul_back(grad_ffn, w_down)
    grad_pre = gelu_pull(grad_active)[0].astype(jnp.bfloat16)
    grad_bias_up = jnp.sum(grad_pre, axis=0, dtype=jnp.float32)
    grad_w_up = matmul_rows(normed_low, grad_pre)
    grad_normed = grad_two + matmul_back(grad_pre, w_up)
    grad_one, grad_gain_one, grad_beta_one = normalize_back(
        grad_normed, unit_one, scale_one, gain_one
    )
    grad_attention = grad_one.astype(jnp.bfloat16)
    grad_bias_out = jnp.sum(grad_attention, axis=0, dtype=jnp.float32)
    grad_gathered = lax.all_gather(grad_attention, "head", axis=0, tiled=True)
    grad_out = matmul_rows(context, grad_gathered).reshape(w_out.shape)
    grad_context = matmul_back(grad_gathered, out_rows).astype(jnp.bfloat16)
    grad_projected = attention_backward(projected, log_total, grad_context, local_heads, SEQ)
    grad_qkv = matmul_rows(gathered, grad_projected).reshape(w_qkv.shape)
    grad_bias_qv = pair_sums(grad_projected, local_heads)
    flat_qkv = w_qkv.reshape(model_width, -1)
    picked = grad_projected
    input_grad = grad_one + lax.psum_scatter(
        matmul_back(picked, flat_qkv).astype(jnp.bfloat16), "head", scatter_dimension=0, tiled=True
    ).astype(jnp.float32)
    grad_qkv, grad_bias_qv, grad_out = (
        lax.psum_scatter(grad_qkv, "dp", scatter_dimension=0, tiled=True),
        lax.psum_scatter(grad_bias_qv, "dp", scatter_dimension=2, tiled=True),
        lax.psum_scatter(grad_out, "dp", scatter_dimension=2, tiled=True),
    )
    shared = lax.psum(
        (
            grad_bias_out,
            grad_gain_one,
            grad_beta_one,
            grad_w_up,
            grad_bias_up,
            grad_w_down,
            grad_bias_down,
            grad_gain_two,
            grad_beta_two,
        ),
        ("dp", "head"),
    )
    return (layer_out, input_grad, grad_qkv, grad_bias_qv, grad_out) + tuple(shared)


def solution(mesh):
    return jax.shard_map(
        shards,
        mesh=mesh,
        in_specs=(
            P(("dp", "head"), None),
            P(("dp", "head"), None),
            P(None, "head", None),
            P("head", None, None),
            P("head", None, None),
            P(),
            P(),
            P(),
            P(),
            P(),
            P(),
            P(),
            P(),
            P(),
        ),
        out_specs=(
            P(("dp", "head"), None),
            P(("dp", "head"), None),
            P("dp", "head", None),
            P("head", None, "dp"),
            P("head", None, "dp"),
            P(),
            P(),
            P(),
            P(),
            P(),
            P(),
            P(),
            P(),
            P(),
        ),
        check_vma=False,
    )
```

profile of v0, /device:TPU:0, one launch (start us, length us, event | category | flops | bytes accessed | tf_op | source)
XLA Modules:
  0.0 859.8 jit_solution(7367107516783642541)
XLA Ops:
  9.0 49.7 %all-gather.3.cloned.1.call-done = bf16[4096,768]{1,0:T(8,128)(2,1)} async-done(((bf16[1024,768]{1,0:T(8,128)(2,1)}), bf16[4096,768]{1,0:T(8,128)(2,1)}) %all-gather.3.cloned.1.call-update) | async-done | bytes 6291472 | tf_op jit(solution)/shard_map/all_gather | solution.py:154
  58.7 8.3 add_convert_fusion.1
  67.0 8.7 %reshape.177 = bf16[8,4,128,3,3,64]{2,1,0,5,4,3:T(4,128)(2,1)} reshape(bf16[4096,576]{0,1:T(8,128)(2,1)} %add_convert_fusion.1) | data formatting | bytes 9437184 | tf_op jit(solution)/shard_map/reshape | solution.py:51
  75.7 6.3 copy.50
  82.0 26.3 %while.22 = (s32[]{:T(128)}, bf16[8,4,128,3,64]{2,1,0,4,3:T(4,128)(2,1)}, f32[8,4,3,128,1]{3,2,1,4,0:T(4,128)}, bf16[8,4,128,3,3,64]{2,5,3,1,4,0:T(8,128)(2,1)}, s32[]{:T(128)}) while((s32[]{:T(128)}, bf16[8,4,128,3,64]{2,1,0,4,3:T(4,128)(2,1)}, f32[8,4,3,128,1]{3,2,1,4,0:T(4,128)}, bf16[8,4,128,3,3,64]{2,5,3,1,4,0:T(8,128)(2,1)}, ...), condition=%wide.region_3.4_spmd, body=%wide.region_0.3_spmd.sunk | while | flops 51804672 | bytes 4773969 | solution.py:110
  116.4 58.0 %reduce-scatter.8.cloned.1.call-done = bf16[1024,768]{1,0:T(8,128)(2,1)} async-done(((bf16[4096,768]{1,0:T(8,128)(2,1)}), bf16[1024,768]{1,0:T(8,128)(2,1)}) %reduce-scatter.8.cloned.1.call-update) | async-done | bytes 1572880 | tf_op jit(solution)/shard_map/reduce_scatter | solution.py:160
  177.5 37.9 %multiply_convert_fusion.1 = (bf16[1024,3072]{1,0:T(8,128)(2,1)S(1)}, f32[1024,3072]{1,0:T(8,128)}, f32[1024,3072]{1,0:T(8,128)}) fusion(f32[3072]{0:T(1024)S(1)} %copy-done.15, bf16[768,3072]{1,0:T(8,128)(2,1)} %param.26, f32[768]{0:T(1024)S(1)} %copy-done.12, f32[768]{0:T(1024)S(1)} %copy-done.11, f32[1024]{0:T(1024)S(1)} %add_rsqrt_fusion.1, ...), kind=kOutput, calls=%fused_computation.39 | convolution fusion | flops 5046534144 | bytes 39351296 | tf_op jit(solution)/shard_map/dot_general | solution.py:172
  215.4 5.6 fusion.42
  227.2 18.7 %convert_reduce_fusion = (f32[3072]{0:T(1024)S(1)}, bf16[1024,3072]{1,0:T(8,128)(2,1)}) fusion(f32[1024,3072]{1,0:T(8,128)} %get-tuple-element.134, bf16[3072,768]{1,0:T(8,128)(2,1)} %param.28, f32[1024,768]{1,0:T(8,128)} %get-tuple-element.130, f32[1024,3072]{1,0:T(8,128)} %get-tuple-element.144, f32[3072]{0:T(1024)S(1)} %copy-done.15), kind=kOutput, calls=%fused_computation.37 | convolution fusion | flops 4886098944 | bytes 39346176 | tf_op jit(solution)/shard_map/dot_general | solution.py:21
  245.8 10.5 %multiply_reduce_fusion.1 = (f32[768]{0:T(1024)S(1)}, f32[1024]{0:T(1024)S(1)}, f32[1024]{0:T(1024)S(1)}, f32[768]{0:T(1024)S(1)}, f32[1024,768]{1,0:T(8,128)S(1)}) fusion(f32[1024]{0:T(1024)S(1)} %add_rsqrt_fusion.1, f32[1024]{0:T(1024)S(1)} %broadcast_multiply_fusion.5, f32[768]{0:T(1024)S(1)} %copy-done.10, bf16[1024,768]{1,0:T(8,128)(2,1)S(1)} %copy-done.2, ...), kind=kOutput, calls=%fused_computation.71 | convolution fusion | flops 4842844160 | bytes 20475904 | tf_op jit(solution)/shard_map/dot_general | solution.py:21
  258.9 46.5 %all-gather.5.cloned.1.call-done = bf16[4096,768]{1,0:T(8,128)(2,1)} async-done(((bf16[1024,768]{1,0:T(8,128)(2,1)}), bf16[4096,768]{1,0:T(8,128)(2,1)}) %all-gather.5.cloned.1.call-update) | async-done | bytes 6291472 | tf_op jit(solution)/shard_map/all_gather | solution.py:193
  305.4 6.1 convolution_convert_fusion.4
  324.2 44.3 %while.23 = (s32[]{:T(128)}, bf16[8,4,128,3,3,64]{2,5,3,1,4,0:T(8,128)(2,1)}, bf16[8,4,128,3,3,64]{2,5,3,1,4,0:T(8,128)(2,1)}, f32[8,4,3,128,1]{3,2,1,4,0:T(4,12...) while((s32[]{:T(128)}, bf16[8,4,128,3,3,64]{2,5,3,1,4,0:T(8,128)(2,1)}, ...), condition=%wide.region_15.16_spmd, body=%wide.region_13.15_spmd.sunk | while | flops 129661440 | bytes 10649693 | solution.py:117
  368.5 8.2 copy.54
  376.6 8.8 %reshape.181 = bf16[4096,576]{0,1:T(8,128)(2,1)} reshape(bf16[8,4,128,3,3,64]{2,1,0,5,4,3:T(4,128)(2,1)} %copy.54) | data formatting | bytes 9437184 | tf_op jit(solution)/shard_map/reshape | solution.py:118
  385.5 9.5 %convolution_convert_fusion.2 = bf16[4096,768]{1,0:T(8,128)(2,1)} fusion(bf16[4096,576]{0,1:T(8,128)(2,1)} %reshape.181, bf16[768,576]{0,1:T(8,128)(2,1)S(1)} %bitcast.143), kind=kOutput, calls=%fused_computation.55 | convolution fusion | flops 3627024384 | bytes 11894784 | tf_op jit(solution)/shard_map/dot_general | solution.py:21
  395.0 11.2 %fusion.32 = f32[3072,768]{1,0:T(8,128)} fusion(bf16[1024,3072]{1,0:T(8,128)(2,1)} %copy-done.18, f32[1024,768]{1,0:T(8,128)} %get-tuple-element.130), kind=kOutput, calls=%fused_computation.101 | convolution fusion | flops 4832624640 | bytes 18874368 | tf_op jit(solution)/shard_map/dot_general | solution.py:15
  406.2 11.5 %fusion.28 = f32[768,3072]{1,0:T(8,128)} fusion(bf16[1024,3072]{1,0:T(8,128)(2,1)} %get-tuple-element.149, f32[768]{0:T(1024)S(1)} %copy-done.12, f32[768]{0:T(1024)S(1)} %copy-done.11, bf16[1024,768]{1,0:T(8,128)(2,1)S(1)} %copy-done.3, bf16[1024,768]{1,0:T(8,128)(2,1)S(1)} %copy-done.1, f32[1024]{0:T(1024)S(1)} %add_rsqrt_fusion.1, ...), kind=kOutput, calls=%fused_computation.88 | convolution fusion | flops 4838916096 | bytes 18891776 | tf_op jit(solution)/shard_map/dot_general | solution.py:15
  417.8 9.2 %fusion.43 = f32[576,768]{1,0:T(8,128)} fusion(bf16[4096,576]{0,1:T(8,128)(2,1)} %reshape.181, bf16[4096,768]{1,0:T(8,128)(2,1)} %all-gather.3.cloned.1.call-done), kind=kOutput, calls=%fused_computation.109 | convolution fusion | flops 3623878656 | bytes 12779520 | tf_op jit(solution)/shard_map/dot_general | solution.py:15
  431.3 41.3 %all-reduce.1 = (f32[768]{0:T(1024)}, f32[768]{0:T(1024)}, f32[768]{0:T(1024)}, f32[3072]{0:T(1024)}, f32[768]{0:T(1024)}, /*index=5*/f32[768]{0:T(1024)}, f32[768]{0:T(1024)}) all-reduce(f32[768]{0:T(1024)S(1)} %get-tuple-element.131, f32[768]{0:T(1024)S(1)} %get-tuple-element.94, ...), channel_id=1, replica_groups=mesh['dp'=8,'head'=4] {'dp','head'}, use_global_device_ids=true, to_apply=%region_22.23 | all-reduce | flops 7680 | bytes 61440 | tf_op jit(solution)/shard_map/psum | solution.py:209
  475.9 22.0 %all-reduce = f32[3,2,64]{2,1,0:T(2,128)S(1)} all-reduce(f32[3,2,64]{2,1,0:T(2,128)S(1)} %copy.56), channel_id=5, replica_groups=mesh['dp'=8,'head'=4] {'dp'}, use_global_device_ids=true, to_apply=%region_19.20.clone | all-reduce | flops 384 | bytes 3072
  505.1 261.7 %all-reduce.5.cloned.1.call-done = (f32[768,3072]{1,0:T(8,128)}, f32[3072,768]{1,0:T(8,128)}) async-done(((f32[768,3072]{1,0:T(8,128)}, f32[3072,768]{1,0:T(8,128)}), (f32[768,3072]{1,0:T(8,128)}, f32[3072,768]{1,0:T(8,128)})) %all-reduce.5.cloned.1.call-update) | async-done | bytes 18874384 | tf_op jit(solution)/shard_map/psum | solution.py:209
  766.8 73.4 %reduce-scatter.12.cloned.1.call-done = f32[96,3,192]{2,0,1:T(8,128)} async-done(((f32[768,3,192]{2,0,1:T(8,128)}), f32[96,3,192]{2,0,1:T(8,128)}) %reduce-scatter.12.cloned.1.call-update) | async-done | bytes 221200 | tf_op jit(solution)/shard_map/reduce_scatter | solution.py:205
  840.2 8.8 %copy.102 = f32[768,3072]{1,0:T(8,128)} copy(f32[768,3072]{1,0:T(8,128)} %get-tuple-element.257) | data formatting | bytes 18874368
  (224 shorter events, 121.9 us)
Async XLA Ops:
  7.2 51.5 %copy-start = (bf16[768,3,192]{0,2,1:T(8,128)(2,1)S(1)}, bf16[768,3,192]{0,2,1:T(8,128)(2,1)}, u32[]{:S(2)}) copy-start(bf16[768,3,192]{0,2,1:T(8,128)(2,1)} %param.20) | copy-start | bytes 2654212
  7.2 51.5 %all-gather.3.cloned.1.call-start = ((), (), s32[]{:S(2)}) async-start(), calls=%async_computation.4 | async-start | bytes 7864320 | tf_op jit(solution)/shard_map/all_gather | solution.py:154
  7.9 166.4 %reduce-scatter.8.cloned.1.call-start = ((), (), s32[]{:S(2)}) async-start(), calls=%async_computation.5 | async-start | bytes 7864320 | tf_op jit(solution)/shard_map/reduce_scatter | solution.py:160
  108.3 2.9 copy-start.8
  111.2 4.6 copy-start.5
  115.8 58.5 %copy-start.1 = (bf16[1024,768]{1,0:T(8,128)(2,1)S(1)}, bf16[1024,768]{1,0:T(8,128)(2,1)}, u32[]{:S(2)}) copy-start(bf16[1024,768]{1,0:T(8,128)(2,1)} %param.18) | copy-start | bytes 4718596
  115.8 58.5 %copy-start.10 = (f32[768]{0:T(1024)S(1)}, f32[768]{0:T(1024)}, u32[]{:S(2)}) copy-start(f32[768]{0:T(1024)} %param.23) | copy-start | bytes 9220
  115.9 61.6 %copy-start.11 = (f32[768]{0:T(1024)S(1)}, f32[768]{0:T(1024)}, u32[]{:S(2)}) copy-start(f32[768]{0:T(1024)} %param.24) | copy-start | bytes 9220
  115.9 61.6 %copy-start.12 = (f32[768]{0:T(1024)S(1)}, f32[768]{0:T(1024)}, u32[]{:S(2)}) copy-start(f32[768]{0:T(1024)} %param.25) | copy-start | bytes 9220
  115.9 61.6 %copy-start.15 = (f32[3072]{0:T(1024)S(1)}, f32[3072]{0:T(1024)}, u32[]{:S(2)}) copy-start(f32[3072]{0:T(1024)} %param.27) | copy-start | bytes 36868
  115.9 189.5 %all-gather.5.cloned.1.call-start = ((), (), s32[]{:S(2)}) async-start(), calls=%async_computation.6 | async-start | bytes 7864320 | tf_op jit(solution)/shard_map/all_gather | solution.py:193
  174.4 41.0 %slice-start = ((s8[4718592]{0:T(1024)(128)(4,1)}), s8[4194304]{0:T(1024)(128)(4,1)S(1)}, s32[]{:S(2)}) async-start(s8[4718592]{0:T(1024)(128)(4,1)} %bitcast.150), calls=%async_computation.11 | async-start | bytes 8388608
  177.5 38.0 %slice-start.1 = ((s8[4718592]{0:T(1024)(128)(4,1)}), s8[524288]{0:T(1024)(128)(4,1)S(1)}, s32[]{:S(2)}) async-start(s8[4718592]{0:T(1024)(128)(4,1)} %bitcast.150), calls=%async_computation.12 | async-start | bytes 1048576
  177.5 38.0 %copy-start.16 = (f32[768]{0:T(1024)S(1)}, f32[768]{0:T(1024)}, u32[]{:S(2)}) copy-start(f32[768]{0:T(1024)} %param.29) | copy-start | bytes 9220
  215.4 5.7 copy-start.18
  221.6 2.6 copy-start.14
  256.4 49.0 %copy-start.9 = (bf16[3,64,768]{2,1,0:T(8,128)(2,1)S(1)}, bf16[3,64,768]{2,1,0:T(8,128)(2,1)}, u32[]{:S(2)}) copy-start(bf16[3,64,768]{2,1,0:T(8,128)(2,1)} %param.22) | copy-start | bytes 884740
  258.8 239.7 %reduce-scatter.14.cloned.1.call-start = ((), (), s32[]{:S(2)}) async-start(), calls=%async_computation.9 | async-start | bytes 884736
  324.1 176.2 %reduce-scatter.10.cloned.1.call-start = ((), (), s32[]{:S(2)}) async-start(), calls=%async_computation.7 | async-start | bytes 7864320 | tf_op jit(solution)/shard_map/reduce_scatter | solution.py:201
  395.0 371.8 %all-reduce.5.cloned.1.call-start = ((), (), s32[]{:S(2)}) async-start(), calls=%async_computation.10 | async-start | bytes 37748736 | tf_op jit(solution)/shard_map/psum | solution.py:209
  395.0 11.2 %copy-start.3 = (bf16[1024,768]{1,0:T(8,128)(2,1)S(1)}, bf16[1024,768]{1,0:T(8,128)(2,1)}, u32[]{:S(2)}) copy-start(bf16[1024,768]{1,0:T(8,128)(2,1)} %reduce-scatter.8.cloned.1.call-done) | copy-start | bytes 4718596
  417.7 422.5 %reduce-scatter.12.cloned.1.call-start = ((), (), s32[]{:S(2)}) async-start(), calls=%async_computation.8 | async-start | bytes 2654208 | tf_op jit(solution)/shard_map/reduce_scatter | solution.py:205
  427.0 3.1 copy-start.17
  840.2 8.8 %copy-start.6 = (f32[3072,768]{1,0:T(8,128)S(1)}, f32[3072,768]{1,0:T(8,128)}, u32[]{:S(2)}) copy-start(f32[3072,768]{1,0:T(8,128)} %get-tuple-element.259) | copy-start | bytes 28311556
  (4 other events, 7.4 us)
Sparse Core Ops, SparseCore 0:
  9.6 49.0 all-gather.2
  116.0 58.3 reduce-scatter.7
  258.9 46.3 all-gather.4
  324.2 62.4 reduce-scatter.13
  395.1 59.0 reduce-scatter.9
  462.2 304.5 all-reduce.4
  771.3 68.9 reduce-scatter.11
where the time goes:
time: 868 us; the launch traced here: 860 us
  waiting for transfers between devices  490 us (56%)
  matrix products  156 us (18%)
  local copies, waits for them, and re-layouts  101 us (12%)
  blocking collectives  63.2 us (7%)
  other arithmetic  32.6 us (4%)
  between operations  15.3 us (2%)
    psum x1, waiting for transfers between devices, shards(): lax.psum((grad_bias_out, grad_gain_one, grad_beta_one, grad_w_up, grad_bi...  262 us
    reduce_scatter x1, waiting for transfers between devices, shards(): lax.psum_scatter(grad_qkv, 'dp', scatter_dimension=0, tiled=True)  73.4 us
    reduce_scatter x1, waiting for transfers between devices, shards(): lax.psum_scatter(jnp.dot(picked, out_rows, preferred_element_type=jnp.flo...  58 us
    all_gather x1, waiting for transfers between devices, shards(): gathered = lax.all_gather(tokens, 'head', axis=0, tiled=True)  49.7 us
    all_gather x1, waiting for transfers between devices, shards(): grad_gathered = lax.all_gather(grad_attention, 'head', axis=0, tiled=True)  46.5 us
    dot_general x4, matrix products, matmul_back(): lax.dot_general(left, right, (((1,), (1,)), ((), ())), preferred_element_...  44.7 us
    psum x1, blocking collectives, shards(): lax.psum((grad_bias_out, grad_gain_one, grad_beta_one, grad_w_up, grad_bi...  41.3 us
    dot_general x1, matrix products, shards(): jnp.dot(normed_low, w_up, preferred_element_type=jnp.float32) + bias_up  37.9 us
  transfers between devices with their start and end apart: 7, of which 5 were waited for; matrix products, arithmetic and copies ran while one was open for 14% of the time, Pallas kernels for 0%

commit v1 on v0

--- a/solution.py
+++ b/solution.py
@@ -1,3 +1,4 @@
+import functools
 import math
 
 import jax
@@ -118,22 +119,112 @@
     return grads.reshape(projected.shape[0], -1)
 
 
-def project(inputs, weight, bias_pair):
-    model_width = weight.shape[0]
-    raw_qkv = jnp.dot(inputs, weight.reshape(model_width, -1), preferred_element_type=jnp.float32)
-    bias_wide = bias_pair.astype(jnp.float32)
-    full_bias = jnp.stack(
-        [bias_wide[:, 0], jnp.zeros_like(bias_wide[:, 0]), bias_wide[:, 1]], axis=1
-    )
-    return (raw_qkv + full_bias.reshape(-1)).astype(jnp.bfloat16)
-
-
-def pair_sums(grad_projected, head_count):
-    column_sums = jnp.sum(grad_projected, axis=0, dtype=jnp.float32).reshape(head_count, 3, -1)
-    return jnp.stack([column_sums[:, 0], column_sums[:, 2]], axis=1)
+AXES = ("dp", "head")
+
+
+class Net:
+    def __init__(self, dp_size, head_size):
+        self.size = dp_size * head_size
+        self.index = lax.axis_index("dp") * head_size + lax.axis_index("head")
+        self.head_bits = [1 << k for k in range(head_size.bit_length() - 1)]
+        self.dp_bits = [head_size << k for k in range(dp_size.bit_length() - 1)]
+
+    def bit(self, mask):
+        return (self.index // mask) % 2
+
+    def swap(self, values, mask):
+        return lax.ppermute(values, AXES, [(i, i ^ mask) for i in range(self.size)])
+
+
+def half(values, which, axis):
+    part = values.shape[axis] // 2
+    return lax.dynamic_slice_in_dim(values, which * part, part, axis)
+
+
+def reduce_half(net, values, mask, axis):
+    own = net.bit(mask)
+    received = net.swap(half(values, 1 - own, axis), mask)
+    kept = half(values, own, axis)
+    return (kept.astype(jnp.float32) + received.astype(jnp.float32)).astype(jnp.bfloat16)
+
+
+def join_half(net, values, mask, axis):
+    own = net.bit(mask)
+    received = net.swap(values, mask)
+    return jnp.where(
+        own == 0,
+        jnp.concatenate([values, received], axis),
+        jnp.concatenate([received, values], axis),
+    )
+
+
+def routes(net):
+    first, second = net.dp_bits[0], net.head_bits[-1]
+    rest = net.head_bits[1:-1] + net.dp_bits[1:]
+    return net.head_bits[0], (first, second), (second, first), rest
+
+
+def reduce_square(net, squares):
+    core, *orders, rest = routes(net)
+    mine = reduce_half(net, squares, core, 0)
+    done = []
+    for color, order in enumerate(orders):
+        part = mine[color]
+        for mask in order:
+            part = reduce_half(net, part, mask, 0)
+        done.append(part)
+    done = jnp.stack(done)
+    for mask in rest:
+        done = reduce_half(net, done, mask, 1)
+    return done
+
+
+def gather_square(net, done):
+    core, *orders, rest = routes(net)
+    for mask in reversed(rest):
+        done = join_half(net, done, mask, 1)
+    parts = []
+    for color, order in enumerate(orders):
+        part = done[color]
+        for mask in reversed(order):
+            part = join_half(net, part, mask, 0)
+        parts.append(part)
+    return join_half(net, jnp.stack(parts), core, 0)
+
+
+def reduce_heads(net, groups, dp_size):
+    for mask in net.head_bits:
+        half_count = groups.shape[0] // 2
+        pairs = groups.reshape((half_count, 2) + groups.shape[1:])
+        received = net.swap(pairs[:, 1], mask)
+        groups = (pairs[:, 0].astype(jnp.float32) + received.astype(jnp.float32)).astype(jnp.bfloat16)
+    rows = groups[0].reshape((dp_size, -1) + groups.shape[2:])
+    for mask in net.dp_bits:
+        count = rows.shape[0] // 2
+        own = net.bit(mask)
+        pairs = rows.reshape((count, 2) + rows.shape[1:])
+        received = net.swap(lax.dynamic_index_in_dim(pairs, 1 - own, 1, False), mask)
+        kept = lax.dynamic_index_in_dim(pairs, own, 1, False)
+        rows = (kept.astype(jnp.float32) + received.astype(jnp.float32)).astype(jnp.bfloat16)
+    return rows[0]
+
+
+def sum_everywhere(net, values):
+    for mask in net.head_bits + net.dp_bits:
+        values = values + net.swap(values, mask)
+    return values
+
+
+def gather_heads(net, values):
+    parts = values[None]
+    for mask in net.head_bits:
+        parts = jnp.concatenate([parts, net.swap(parts, mask)], 0)
+    return parts
 
 
 def shards(
+    dp_size,
+    head_size,
     tokens,
     cotangent,
     w_qkv,
@@ -149,22 +240,25 @@
     gain_two,
     beta_two,
 ):
+    net = Net(dp_size, head_size)
     model_width = tokens.shape[1]
     local_heads = w_qkv.shape[1]
-    gathered = lax.all_gather(tokens, "head", axis=0, tiled=True)
-    projected = project(gathered, w_qkv, bias_qv)
-    context, log_total = attention_forward(projected, local_heads, SEQ)
+    heads = local_heads * head_size
+    head_dim = w_qkv.shape[2] // 3
+    w_qkv = gather_heads(net, w_qkv.reshape(model_width, -1))
+    bias_qv = gather_heads(net, bias_qv)
+    w_out = gather_heads(net, w_out.reshape(-1, model_width))
+    bias_wide = bias_qv.astype(jnp.float32)
+    full_bias = jnp.stack(
+        [bias_wide[:, :, 0], jnp.zeros_like(bias_wide[:, :, 0]), bias_wide[:, :, 1]], axis=2
+    ).reshape(-1)
+    flat_qkv = jnp.swapaxes(w_qkv, 0, 1).reshape(model_width, -1)
     out_rows = w_out.reshape(-1, model_width)
-    picked = context
-    attention = (
-        lax.psum_scatter(
-            jnp.dot(picked, out_rows, preferred_element_type=jnp.float32).astype(jnp.bfloat16),
-            "head",
-            scatter_dimension=0,
-            tiled=True,
-        ).astype(jnp.float32)
-        + bias_out
-    )
+    projected = (
+        jnp.dot(tokens, flat_qkv, preferred_element_type=jnp.float32) + full_bias
+    ).astype(jnp.bfloat16)
+    context, log_total = attention_forward(projected, heads, SEQ)
+    attention = jnp.dot(context, out_rows, preferred_element_type=jnp.float32) + bias_out
     normed_one, unit_one, scale_one = normalize(
         tokens.astype(jnp.float32) + attention, gain_one, beta_one
     )
@@ -179,53 +273,96 @@
     grad_two, grad_gain_two, grad_beta_two = normalize_back(upstream, unit_two, scale_two, gain_two)
     grad_ffn = grad_two.astype(jnp.bfloat16)
     grad_bias_down = jnp.sum(grad_ffn, axis=0, dtype=jnp.float32)
-    grad_w_down = matmul_rows(activated, grad_ffn)
+    grad_w_down = matmul_rows(activated, grad_ffn).astype(jnp.bfloat16)
+    down_part = reduce_square(net, grad_w_down.reshape(4, -1, model_width))
     grad_active = matmul_back(grad_ffn, w_down)
     grad_pre = gelu_pull(grad_active)[0].astype(jnp.bfloat16)
     grad_bias_up = jnp.sum(grad_pre, axis=0, dtype=jnp.float32)
-    grad_w_up = matmul_rows(normed_low, grad_pre)
+    quarter = grad_pre.shape[1] // 4
+    grad_w_up = jnp.stack(
+        [
+            matmul_rows(normed_low, grad_pre[:, k * quarter : (k + 1) * quarter]).astype(jnp.bfloat16)
+            for k in range(4)
+        ]
+    )
+    up_part = reduce_square(net, grad_w_up)
     grad_normed = grad_two + matmul_back(grad_pre, w_up)
     grad_one, grad_gain_one, grad_beta_one = normalize_back(
         grad_normed, unit_one, scale_one, gain_one
     )
     grad_attention = grad_one.astype(jnp.bfloat16)
     grad_bias_out = jnp.sum(grad_attention, axis=0, dtype=jnp.float32)
-    grad_gathered = lax.all_gather(grad_attention, "head", axis=0, tiled=True)
-    grad_out = matmul_rows(context, grad_gathered).reshape(w_out.shape)
-    grad_context = matmul_back(grad_gathered, out_rows).astype(jnp.bfloat16)
-    grad_projected = attention_backward(projected, log_total, grad_context, local_heads, SEQ)
-    grad_qkv = matmul_rows(gathered, grad_projected).reshape(w_qkv.shape)
-    grad_bias_qv = pair_sums(grad_projected, local_heads)
-    flat_qkv = w_qkv.reshape(model_width, -1)
-    picked = grad_projected
-    input_grad = grad_one + lax.psum_scatter(
-        matmul_back(picked, flat_qkv).astype(jnp.bfloat16), "head", scatter_dimension=0, tiled=True
-    ).astype(jnp.float32)
-    grad_qkv, grad_bias_qv, grad_out = (
-        lax.psum_scatter(grad_qkv, "dp", scatter_dimension=0, tiled=True),
-        lax.psum_scatter(grad_bias_qv, "dp", scatter_dimension=2, tiled=True),
-        lax.psum_scatter(grad_out, "dp", scatter_dimension=2, tiled=True),
-    )
-    shared = lax.psum(
-        (
-            grad_bias_out,
-            grad_gain_one,
-            grad_beta_one,
-            grad_w_up,
-            grad_bias_up,
-            grad_w_down,
-            grad_bias_down,
-            grad_gain_two,
-            grad_beta_two,
-        ),
-        ("dp", "head"),
-    )
-    return (layer_out, input_grad, grad_qkv, grad_bias_qv, grad_out) + tuple(shared)
+    grad_context = matmul_back(grad_attention, out_rows).astype(jnp.bfloat16)
+    grad_projected = attention_backward(projected, log_total, grad_context, heads, SEQ)
+    input_grad = grad_one + matmul_back(grad_projected, flat_qkv)
+    wide = 3 * local_heads * head_dim
+    deep = local_heads * head_dim
+    groups = jnp.stack(
+        [
+            jnp.concatenate(
+                [
+                    matmul_rows(tokens, grad_projected[:, k * wide : (k + 1) * wide]),
+                    matmul_rows(grad_attention, context[:, k * deep : (k + 1) * deep]),
+                ],
+                axis=1,
+            ).astype(jnp.bfloat16)
+            for k in range(head_size)
+        ]
+    )
+    attn_part = reduce_heads(net, groups, dp_size).astype(jnp.float32)
+    rows = attn_part.shape[0]
+    grad_qkv = attn_part[:, :wide].reshape(rows, local_heads, 3 * head_dim)
+    grad_out = attn_part[:, wide:].T.reshape(local_heads, head_dim, rows)
+    sums = jnp.sum(grad_projected, axis=0, dtype=jnp.float32).reshape(
+        head_size, local_heads, 3, head_dim
+    )
+    pair = jnp.stack([sums[:, :, 0], sums[:, :, 2]], axis=2)
+    head_index = lax.axis_index("head")
+    pair = jnp.stack(
+        [lax.dynamic_index_in_dim(pair, head_index ^ k, 0, False) for k in range(head_size)]
+    )
+    small = (
+        grad_bias_out,
+        grad_gain_one,
+        grad_beta_one,
+        grad_bias_up,
+        grad_bias_down,
+        grad_gain_two,
+        grad_beta_two,
+        pair.reshape(-1),
+    )
+    total = sum_everywhere(net, jnp.concatenate(small).reshape(-1, 128)).reshape(-1)
+    split = []
+    at = 0
+    for part in small:
+        split.append(total[at : at + part.size])
+        at += part.size
+    pair = lax.dynamic_index_in_dim(split[7].reshape(pair.shape), head_index, 0, False)
+    cut = head_dim // dp_size
+    grad_bias_qv = lax.dynamic_slice_in_dim(pair, lax.axis_index("dp") * cut, cut, 2)
+    full_down = gather_square(net, down_part).reshape(w_down.shape).astype(jnp.float32)
+    full_up = jnp.swapaxes(gather_square(net, up_part), 0, 1).reshape(w_up.shape).astype(jnp.float32)
+    return (
+        layer_out,
+        input_grad,
+        grad_qkv,
+        grad_bias_qv,
+        grad_out,
+        split[0],
+        split[1],
+        split[2],
+        full_up,
+        split[3],
+        full_down,
+        split[4],
+        split[5],
+        split[6],
+    )
 
 
 def solution(mesh):
     return jax.shard_map(
-        shards,
+        functools.partial(shards, mesh.shape["dp"], mesh.shape["head"]),
         mesh=mesh,
         in_specs=(
             P(("dp", "head"), None),

time: 868 us -> 496 us (0.57)
  waiting for transfers between devices: 490 us -> 117 us
  blocking collectives: 63.2 us -> 0 us
  starting transfers between devices: 0.75 us -> 45.9 us
  other arithmetic: 32.6 us -> 65.8 us
  matrix products: 156 us -> 136 us
  local copies, waits for them, and re-layouts: 101 us -> 120 us
  between operations: 15.3 us -> 2.11 us
    psum x1 -> x0, waiting for transfers between devices: 262 us -> none  [shards(): lax.psum((grad_bias_out, grad_gain_one, grad_beta_one, grad_w_up, grad_bi...]
    reduce_scatter x3 -> x0, waiting for transfers between devices: 131 us -> none  [the longest x1 73.4 us: shards(): lax.psum_scatter(grad_qkv, 'dp', scatter_dimension=0, tiled=True)]
    ppermute x0 -> x44, waiting for transfers between devices: none -> 117 us  [swap(): return lax.ppermute(values, AXES, [(i, i ^ mask) for i in range(self.size)])]
    all_gather x2 -> x0, waiting for transfers between devices: 96.2 us -> none  [the longest x1 49.7 us: shards(): gathered = lax.all_gather(tokens, 'head', axis=0, tiled=True)]
    ppermute x0 -> x44, starting transfers between devices: none -> 45.9 us  [swap(): return lax.ppermute(values, AXES, [(i, i ^ mask) for i in range(self.size)])]
    psum x1 -> x0, blocking collectives: 41.3 us -> none  [shards(): lax.psum((grad_bias_out, grad_gain_one, grad_beta_one, grad_w_up, grad_bi...]
    convert_element_type x0 -> x18, other arithmetic: none -> 22 us  [the longest x10 7.63 us: reduce_half(): (kept.astype(jnp.float32) + received.astype(jnp.float32)).astype(jnp.bflo...]
    unnamed x1 -> x0, blocking collectives: 22 us -> none
  transfers between devices with their start and end apart: 7 -> 44, of which waited for: 5 -> 19; matrix products, arithmetic and copies ran while one was open for 14% -> 17% of each run, Pallas kernels for 0% -> 0%
where the time goes in v1:
time: 496 us; the launch traced here: 487 us
  matrix products  136 us (27%)
  local copies, waits for them, and re-layouts  120 us (24%)
  waiting for transfers between devices  117 us (24%)
  other arithmetic  65.8 us (13%)
  starting transfers between devices  45.9 us (9%)
    ppermute x44, waiting for transfers between devices, swap(): return lax.ppermute(values, AXES, [(i, i ^ mask) for i in range(self.size)])  117 us
    ppermute x44, starting transfers between devices, swap(): return lax.ppermute(values, AXES, [(i, i ^ mask) for i in range(self.size)])  45.9 us
    unnamed x133, local copies, waits for them, and re-layouts  42.5 us
    dot_general x1, matrix products, shards(): jnp.dot(normed_low, w_up, preferred_element_type=jnp.float32) + bias_up  36.8 us
    dot_general x4, matrix products, matmul_back(): lax.dot_general(left, right, (((1,), (1,)), ((), ())), preferred_element_...  35.9 us
    dot_general x13, matrix products, matmul_rows(): lax.dot_general(left, right, (((0,), (0,)), ((), ())), preferred_element_...  35.4 us
  transfers between devices with their start and end apart: 44, of which 19 were waited for; matrix products, arithmetic and copies ran while one was open for 17% of the time, Pallas kernels for 0%

profile of v1, /device:TPU:0, one launch (start us, length us, event | category | flops | bytes accessed | tf_op | source)
XLA Modules:
  0.0 486.5 jit_solution(7121121261083342324)
XLA Ops:
  18.0 42.8 %collective-permute-done.3 = bf16[2,3,2,64]{3,2,1,0:T(2,128)(2,1)S(1)} collective-permute-done((bf16[2,3,2,64]{3,2,1,0:T(2,128)(2,1)S(1)}, bf16[2,3,2,64]{3,2,1,0:T(2,128)(2,1)S(1)}, u32[]{:S(2)}, u32[]{:S(2)}) %collective-permute-start.3) | collective-permute-done | bytes 1568 | tf_op jit(solution)/shard_map/ppermute | solution.py:136
  66.8 5.6 %fusion.28 = bf16[1024,2304]{0,1:T(8,128)(2,1)} fusion(bf16[768,2304]{0,1:T(8,128)(2,1)S(1)} %bitcast.298, bf16[1024,768]{1,0:T(8,128)(2,1)S(1)} %copy-done.17, f32[2304]{0:T(1024)S(1)} %add.323), kind=kOutput, calls=%fused_computation.61 | convolution fusion | flops 3628597248 | bytes 9839616 | tf_op jit(solution)/shard_map/dot_general | solution.py:258
  72.4 8.7 %reshape.802 = bf16[2,4,128,12,3,64]{2,1,0,5,4,3:T(4,128)(2,1)} reshape(bf16[1024,2304]{0,1:T(8,128)(2,1)} %fusion.28) | data formatting | bytes 9437184 | tf_op jit(solution)/shard_map/reshape | solution.py:52
  81.1 5.7 %copy.120 = bf16[2,4,128,12,3,64]{2,5,3,1,4,0:T(8,128)(2,1)} copy(bf16[2,4,128,12,3,64]{2,1,0,5,4,3:T(4,128)(2,1)} %reshape.802) | data formatting | bytes 9437184 | tf_op jit(solution)/shard_map/while | solution.py:111
  86.8 12.1 %while.22 = (s32[]{:T(128)}, bf16[2,4,128,12,64]{2,1,0,4,3:T(4,128)(2,1)}, f32[2,4,12,128,1]{3,2,1,4,0:T(8,128)S(1)}, bf16[2,4,128,12,3,64]{2,5,3,1,4,0:T(8,128)(2,1)}, s32[]{:T(128)}) while((s32[]{:T(128)}, bf16[2,4,128,12,64]{2,1,0,4,3:T(4,128)(2,1)}, f32[2,4,12,128,1]{3,2,1,4,0:T(8,128)S(1)}, bf16[2,4,128,12,3,64]{2,5,3,1,4,0:T(8,128)(2,1)}, ...), condition=%wide.region_3.4_spmd, body=%wide.region_0.3_spmd.sunk | while | flops 208791552 | bytes 19112516 | solution.py:111
  107.9 36.8 %multiply_convert_fusion.3 = (bf16[1024,3072]{1,0:T(8,128)(2,1)S(1)}, f32[1024,3072]{1,0:T(8,128)}, f32[1024,3072]{1,0:T(8,128)}) fusion(f32[3072]{0:T(1024)S(1)} %copy-done.48, bf16[1024,768]{0,1:T(8,128)(2,1)S(1)} %fusion.37, bf16[768,3072]{1,0:T(8,128)(2,1)} %param.26), kind=kOutput, calls=%fused_computation.43 | convolution fusion | flops 5039456256 | bytes 37761024 | tf_op jit(solution)/shard_map/dot_general | solution.py:266
  144.8 6.0 %fusion.120 = (f32[1024]{0:T(1024)S(1)}, f32[1024,768]{0,1:T(8,128)S(1)}) fusion(f32[768]{0:T(1024)S(1)} %copy-done.50, bf16[1024,3072]{1,0:T(8,128)(2,1)S(1)} %get-tuple-element.212, bf16[3072,768]{1,0:T(8,128)(2,1)S(1)} %bitcast.324, f32[768]{0:T(1024)S(1)} %copy-done.46, f32[768]{0:T(1024)S(1)} %copy-done.38, f32[1024]{0:T(1024)S(1)} %add_rsqrt_fusion.1, ...), kind=kOutput, calls=%fused_computation.271 | convolution fusion | flops 4837342208 | bytes 17323008 | tf_op jit(solution)/shard_map/dot_general | solution.py:269
  157.5 6.9 %convolution_convert_fusion = bf16[3072,768]{1,0:T(8,128)(2,1)} fusion(bf16[1024,3072]{1,0:T(8,128)(2,1)S(1)} %get-tuple-element.212, bf16[1024,768]{0,1:T(8,128)(2,1)S(1)} %get-tuple-element.209), kind=kOutput, calls=%fused_computation.60 | convolution fusion | flops 4834197504 | bytes 12582912 | tf_op jit(solution)/shard_map/dot_general | solution.py:16
  164.5 19.2 %convert_reduce_fusion = (f32[3072]{0:T(1024)}, bf16[1024,3072]{1,0:T(8,128)(2,1)}) fusion(f32[1024,3072]{1,0:T(8,128)} %get-tuple-element.213, bf16[1024,768]{0,1:T(8,128)(2,1)} %copy-done.23, bf16[3072,768]{1,0:T(8,128)(2,1)} %param.28, f32[1024,3072]{1,0:T(8,128)} %get-tuple-element.245, f32[3072]{0:T(1024)S(1)} %copy-done.48), kind=kOutput, calls=%fused_computation.41 | convolution fusion | flops 4885312512 | bytes 37773312 | tf_op jit(solution)/shard_map/dot_general | solution.py:22
  195.4 7.2 %multiply_reduce_fusion.2 = (f32[768]{0:T(1024)}, f32[1024]{0:T(1024)S(1)}, f32[1024]{0:T(1024)S(1)}, f32[768]{0:T(1024)}, f32[1024,768]{0,1:T(8,128)S(1)}) fusion(f32[1024,768]{0,1:T(8,128)S(1)} %get-tuple-element.244, f32[1024]{0:T(1024)S(1)} %add_rsqrt_fusion.1, f32[1024]{0:T(1024)S(1)} %broadcast_multiply_fusion.5, f32[768]{0:T(1024)S(1)} %copy-done.38, ...), kind=kOutput, calls=%fused_computation.83 | convolution fusion | flops 4845989888 | bytes 22065152 | tf_op jit(solution)/shard_map/dot_general | solution.py:22
  217.8 21.4 %while.23 = (s32[]{:T(128)}, bf16[2,4,128,12,3,64]{2,5,3,1,4,0:T(8,128)(2,1)}, bf16[2,4,128,12,3,64]{2,5,3,1,4,0:T(8,128)(2,1)}, f32[2,4,12,128,1]{3,2,1,4,0:T(8...) while((s32[]{:T(128)}, bf16[2,4,128,12,3,64]{2,5,3,1,4,0:T(8,128)(2,1)}, ...), condition=%wide.region_14.15_spmd, body=%wide.region_12.14_spmd.sunk | while | flops 521791488 | bytes 48939628 | solution.py:118
  242.3 9.0 %copy.128 = bf16[2,4,128,12,3,64]{2,1,0,5,4,3:T(4,128)(2,1)} copy(bf16[2,4,128,12,3,64]{2,5,3,1,4,0:T(8,128)(2,1)} %get-tuple-element.66) | data formatting | bytes 9437184 | tf_op jit(solution)/shard_map/while | solution.py:118
  251.3 8.7 %reshape.806 = bf16[1024,2304]{0,1:T(8,128)(2,1)} reshape(bf16[2,4,128,12,3,64]{2,1,0,5,4,3:T(4,128)(2,1)} %copy.128) | data formatting | bytes 9437184 | tf_op jit(solution)/shard_map/reshape | solution.py:119
  326.7 6.3 %collective-permute-done.33 = bf16[384,768]{1,0:T(8,128)(2,1)S(1)} collective-permute-done((bf16[384,768]{1,0:T(8,128)(2,1)S(1)}, bf16[384,768]{1,0:T(8,128)(2,1)S(1)}, u32[]{:S(2)}, u32[]{:S(2)}) %collective-permute-start.33) | collective-permute-done | bytes 589856 | tf_op jit(solution)/shard_map/ppermute | solution.py:136
  336.5 9.1 %collective-permute-done.19 = bf16[384,768]{1,0:T(8,128)(2,1)S(1)} collective-permute-done((bf16[384,768]{1,0:T(8,128)(2,1)S(1)}, bf16[384,768]{1,0:T(8,128)(2,1)S(1)}, u32[]{:S(2)}, u32[]{:S(2)}) %collective-permute-start.19) | collective-permute-done | bytes 589856 | tf_op jit(solution)/shard_map/ppermute | solution.py:136
  357.1 6.4 %collective-permute-done.35 = bf16[2,96,768]{2,1,0:T(8,128)(2,1)S(1)} collective-permute-done((bf16[2,96,768]{2,1,0:T(8,128)(2,1)S(1)}, bf16[2,96,768]{2,1,0:T(8,128)(2,1)S(1)}, u32[]{:S(2)}, u32[]{:S(2)}) %collective-permute-start.35) | collective-permute-done | bytes 294944 | tf_op jit(solution)/shard_map/ppermute | solution.py:136
  365.5 9.5 %collective-permute-done.36 = bf16[2,48,768]{2,1,0:T(8,128)(2,1)S(1)} collective-permute-done((bf16[2,48,768]{2,1,0:T(8,128)(2,1)S(1)}, bf16[2,48,768]{2,1,0:T(8,128)(2,1)S(1)}, u32[]{:S(2)}, u32[]{:S(2)}) %collective-permute-start.36) | collective-permute-done | bytes 147488 | tf_op jit(solution)/shard_map/ppermute | solution.py:136
  384.2 6.5 %convolution_add_fusion.1 = f32[1024,768]{0,1:T(8,128)} fusion(bf16[1024,2304]{0,1:T(8,128)(2,1)S(1)} %bitcast.294, bf16[768,2304]{0,1:T(8,128)(2,1)S(1)} %bitcast.299, f32[1024]{0:T(1024)S(1)} %copy-done.40, f32[1024,768]{0,1:T(8,128)S(1)} %get-tuple-element.244, f32[1024]{0:T(1024)S(1)} %broadcast_multiply_fusion.5, f32[1024]{0:T(1024)S(1)} %copy-done.42, ...), kind=kOutput, calls=%fused_computation.104 | convolution fusion | flops 3630170112 | bytes 17714176 | tf_op jit(solution)/shard_map/dot_general | solution.py:22
  417.1 6.2 %collective-permute-done.40 = bf16[384,768]{1,0:T(8,128)(2,1)S(1)} collective-permute-done((bf16[384,768]{1,0:T(8,128)(2,1)S(1)}, bf16[384,768]{1,0:T(8,128)(2,1)S(1)}, u32[]{:S(2)}, u32[]{:S(2)}) %collective-permute-start.40) | collective-permute-done | bytes 589856 | tf_op jit(solution)/shard_map/ppermute | solution.py:136
  440.6 4.8 collective-permute-done.26
  455.8 4.8 bitcast_convert_fusion
  460.6 6.4 %convert_bitcast_fusion = f32[768,4,768]{2,0,1:T(8,128)} fusion(bf16[2,768,768]{2,1,0:T(8,128)(2,1)} %collective-permute-done.29, bf16[1,768,768]{2,1,0:T(8,128)(2,1)S(1)} %copy-done.7, bf16[1,768,768]{2,1,0:T(8,128)(2,1)S(1)} %copy-done.5, pred[]{:T(512)S(6)} %eq.56), kind=kLoop, calls=%fused_computation.57 | loop fusion | flops 14155776 | bytes 14155777 | tf_op jit(solution)/shard_map/convert_element_type | solution.py:344
  466.9 9.5 %copy.135 = f32[768,4,768]{0,2,1:T(8,128)} copy(f32[768,4,768]{2,0,1:T(8,128)} %convert_bitcast_fusion) | data formatting | bytes 18874368 | tf_op jit(solution)/shard_map/convert_element_type | solution.py:344
  476.5 9.6 %copy.139 = f32[768,3072]{1,0:T(8,128)} copy(f32[768,3072]{0,1:T(8,128)} %bitcast.285) | data formatting | bytes 18874368
  (377 shorter events, 248.5 us)
Async XLA Ops:
  6.0 57.2 %collective-permute-start.1 = (bf16[2,768,576]{1,2,0:T(8,128)(2,1)}, bf16[2,768,576]{1,2,0:T(8,128)(2,1)}, u32[]{:S(2)}, u32[]{:S(2)}) collective-permute-start(bf16[2,768,576]{1,2,0:T(8,128)(2,1)} %pad_maximum_fusion.4), channel_id=1, source_target_pairs={{0,2},{1,3},{2,0},{3,1},{4,6},{5,7},{6,4},{7,5},{8,10},{9,11},{10,... | collective-permute-start | bytes 5308424 | tf_op jit(solution)/shard_map/ppermute | solution.py:136
  10.5 50.4 %collective-permute-start.5 = (bf16[2,192,768]{2,1,0:T(8,128)(2,1)S(1)}, bf16[2,192,768]{2,1,0:T(8,128)(2,1)}, u32[]{:S(2)}, u32[]{:S(2)}) collective-permute-start(bf16[2,192,768]{2,1,0:T(8,128)(2,1)S(1)} %pad_maximum_fusion.6), channel_id=1, source_target_pairs={{0,2},{1,3},{2,0},{3,1},{4,6},{5,7},{6,4},{7,5},{8,10},{9,11},{10,... | collective-permute-start | bytes 1769480 | tf_op jit(solution)/shard_map/ppermute | solution.py:136
  10.6 50.1 %collective-permute-start.3 = (bf16[2,3,2,64]{3,2,1,0:T(2,128)(2,1)S(1)}, bf16[2,3,2,64]{3,2,1,0:T(2,128)(2,1)S(1)}, u32[]{:S(2)}, u32[]{:S(2)}) collective-permute-start(bf16[2,3,2,64]{3,2,1,0:T(2,128)(2,1)S(1)} %pad_maximum_fusion.9), channel_id=1, source_target_pairs={{0,2},{1,3},{2,0},{3,1},{4,6},{5,7},{6,4},{7,5},{8,10},{9,11},{10,... | collective-permute-start | bytes 4616 | tf_op jit(solution)/shard_map/ppermute | solution.py:136
  269.6 43.9 %collective-permute-start.30 = (bf16[2,768,768]{2,1,0:T(8,128)(2,1)}, bf16[2,768,768]{2,1,0:T(8,128)(2,1)}, u32[]{:S(2)}, u32[]{:S(2)}) collective-permute-start(bf16[2,768,768]{2,1,0:T(8,128)(2,1)} %constant_dynamic-slice_fusion.4), channel_id=1, source_target_pairs={{0,1},{1,0},{2,3},{3,2},{4,5},{5,4},{6,7},{7,6},{8,9},{9,8},{10,11... | collective-permute-start | bytes 7077896 | tf_op jit(solution)/shard_map/ppermute | solution.py:136
  275.6 44.3 %collective-permute-start.16 = (bf16[2,768,768]{2,1,0:T(8,128)(2,1)}, bf16[2,768,768]{2,1,0:T(8,128)(2,1)}, u32[]{:S(2)}, u32[]{:S(2)}) collective-permute-start(bf16[2,768,768]{2,1,0:T(8,128)(2,1)} %constant_dynamic-slice_fusion.8), channel_id=1, source_target_pairs={{0,1},{1,0},{2,3},{3,2},{4,5},{5,4},{6,7},{7,6},{8,9},{9,8},{10,11... | collective-permute-start | bytes 7077896 | tf_op jit(solution)/shard_map/ppermute | solution.py:136
  279.3 17.4 %collective-permute-start.11 = (f32[72,128]{1,0:T(8,128)S(1)}, f32[72,128]{1,0:T(8,128)S(1)}, u32[]{:S(2)}, u32[]{:S(2)}) collective-permute-start(f32[72,128]{1,0:T(8,128)S(1)} %bitcast.317), channel_id=1, source_target_pairs={{0,1},{1,0},{2,3},{3,2},{4,5},{5,4},{6,7},{7,6},{8,9},{9,8},{10,11... | collective-permute-start | bytes 110600 | tf_op jit(solution)/shard_map/ppermute | solution.py:136
  296.7 26.9 %collective-permute-start.6 = (bf16[2,768,768]{2,1,0:T(8,128)(2,1)}, bf16[2,768,768]{2,1,0:T(8,128)(2,1)}, u32[]{:S(2)}, u32[]{:S(2)}) collective-permute-start(bf16[2,768,768]{2,1,0:T(8,128)(2,1)} %bitcast.304), channel_id=1, source_target_pairs={{0,1},{1,0},{2,3},{3,2},{4,5},{5,4},{6,7},{7,6},{8,9},{9,8},{10,11... | collective-permute-start | bytes 7077896 | tf_op jit(solution)/shard_map/ppermute | solution.py:136
  310.9 86.3 %collective-permute-start.15 = (f32[72,128]{1,0:T(8,128)S(1)}, f32[72,128]{1,0:T(8,128)S(1)}, u32[]{:S(2)}, u32[]{:S(2)}) collective-permute-start(f32[72,128]{1,0:T(8,128)S(1)} %add.364), channel_id=1, source_target_pairs={{0,16},{1,17},{2,18},{3,19},{4,20},{5,21},{6,22},{7,23},{8,24},{9,... | collective-permute-start | bytes 110600 | tf_op jit(solution)/shard_map/ppermute | solution.py:136
  316.7 16.3 %collective-permute-start.33 = (bf16[384,768]{1,0:T(8,128)(2,1)S(1)}, bf16[384,768]{1,0:T(8,128)(2,1)S(1)}, u32[]{:S(2)}, u32[]{:S(2)}) collective-permute-start(bf16[384,768]{1,0:T(8,128)(2,1)S(1)} %dynamic-slice_bitcast_fusion.3), channel_id=1, source_target_pairs={{0,2},{1,3},{2,0},{3,1},{4,6},{5,7},{6,4},{7,5},{8,10},{9,11},{10,... | collective-permute-start | bytes 1769480 | tf_op jit(solution)/shard_map/ppermute | solution.py:136
  318.3 16.5 %collective-permute-start.31 = (bf16[384,768]{1,0:T(8,128)(2,1)S(1)}, bf16[384,768]{1,0:T(8,128)(2,1)S(1)}, u32[]{:S(2)}, u32[]{:S(2)}) collective-permute-start(bf16[384,768]{1,0:T(8,128)(2,1)S(1)} %dynamic-slice_bitcast_fusion.4), channel_id=1, source_target_pairs={{0,4},{1,5},{2,6},{3,7},{4,0},{5,1},{6,2},{7,3},{8,12},{9,13},{10,... | collective-permute-start | bytes 1769480 | tf_op jit(solution)/shard_map/ppermute | solution.py:136
  323.0 22.6 %collective-permute-start.19 = (bf16[384,768]{1,0:T(8,128)(2,1)S(1)}, bf16[384,768]{1,0:T(8,128)(2,1)S(1)}, u32[]{:S(2)}, u32[]{:S(2)}) collective-permute-start(bf16[384,768]{1,0:T(8,128)(2,1)S(1)} %dynamic-slice_bitcast_fusion.5), channel_id=1, source_target_pairs={{0,2},{1,3},{2,0},{3,1},{4,6},{5,7},{6,4},{7,5},{8,10},{9,11},{10,... | collective-permute-start | bytes 1769480 | tf_op jit(solution)/shard_map/ppermute | solution.py:136
  323.7 23.8 %collective-permute-start.17 = (bf16[384,768]{1,0:T(8,128)(2,1)S(1)}, bf16[384,768]{1,0:T(8,128)(2,1)S(1)}, u32[]{:S(2)}, u32[]{:S(2)}) collective-permute-start(bf16[384,768]{1,0:T(8,128)(2,1)S(1)} %dynamic-slice_bitcast_fusion.6), channel_id=1, source_target_pairs={{0,4},{1,5},{2,6},{3,7},{4,0},{5,1},{6,2},{7,3},{8,12},{9,13},{10,... | collective-permute-start | bytes 1769480 | tf_op jit(solution)/shard_map/ppermute | solution.py:136
  333.2 19.9 %collective-permute-start.34 = (bf16[192,768]{1,0:T(8,128)(2,1)S(1)}, bf16[192,768]{1,0:T(8,128)(2,1)S(1)}, u32[]{:S(2)}, u32[]{:S(2)}) collective-permute-start(bf16[192,768]{1,0:T(8,128)(2,1)S(1)} %constant_dynamic-slice_fusion.2), channel_id=1, source_target_pairs={{0,4},{1,5},{2,6},{3,7},{4,0},{5,1},{6,2},{7,3},{8,12},{9,13},{10,... | collective-permute-start | bytes 884744 | tf_op jit(solution)/shard_map/ppermute | solution.py:136
  335.0 18.2 %collective-permute-start.32 = (bf16[192,768]{1,0:T(8,128)(2,1)S(1)}, bf16[192,768]{1,0:T(8,128)(2,1)S(1)}, u32[]{:S(2)}, u32[]{:S(2)}) collective-permute-start(bf16[192,768]{1,0:T(8,128)(2,1)S(1)} %constant_dynamic-slice_fusion.3), channel_id=1, source_target_pairs={{0,2},{1,3},{2,0},{3,1},{4,6},{5,7},{6,4},{7,5},{8,10},{9,11},{10,... | collective-permute-start | bytes 884744 | tf_op jit(solution)/shard_map/ppermute | solution.py:136
  356.5 18.6 %collective-permute-start.21 = (bf16[2,96,768]{2,1,0:T(8,128)(2,1)S(1)}, bf16[2,96,768]{2,1,0:T(8,128)(2,1)S(1)}, u32[]{:S(2)}, u32[]{:S(2)}) collective-permute-start(bf16[2,96,768]{2,1,0:T(8,128)(2,1)S(1)} %fusion.101), channel_id=1, source_target_pairs={{0,8},{1,9},{2,10},{3,11},{4,12},{5,13},{6,14},{7,15},{8,0},{9,1},... | collective-permute-start | bytes 884744 | tf_op jit(solution)/shard_map/ppermute | solution.py:136
  365.0 37.7 %collective-permute-start.7 = (bf16[1,768,768]{2,1,0:T(8,128)(2,1)}, bf16[1,768,768]{2,1,0:T(8,128)(2,1)}, u32[]{:S(2)}, u32[]{:S(2)}) collective-permute-start(bf16[1,768,768]{2,1,0:T(8,128)(2,1)} %slice_bitcast_fusion.14), channel_id=1, source_target_pairs={{0,2},{1,3},{2,0},{3,1},{4,6},{5,7},{6,4},{7,5},{8,10},{9,11},{10,... | collective-permute-start | bytes 3538952 | tf_op jit(solution)/shard_map/ppermute | solution.py:136
  375.9 21.4 %collective-permute-start.22 = (bf16[2,48,768]{2,1,0:T(8,128)(2,1)}, bf16[2,48,768]{2,1,0:T(8,128)(2,1)}, u32[]{:S(2)}, u32[]{:S(2)}) collective-permute-start(bf16[2,48,768]{2,1,0:T(8,128)(2,1)} %constant_dynamic-slice_fusion.5), channel_id=1, source_target_pairs={{0,16},{1,17},{2,18},{3,19},{4,20},{5,21},{6,22},{7,23},{8,24},{9,... | collective-permute-start | bytes 442376 | tf_op jit(solution)/shard_map/ppermute | solution.py:136
  384.2 15.0 %collective-permute-start.38 = (bf16[2,96,768]{2,1,0:T(8,128)(2,1)}, bf16[2,96,768]{2,1,0:T(8,128)(2,1)}, u32[]{:S(2)}, u32[]{:S(2)}) collective-permute-start(bf16[2,96,768]{2,1,0:T(8,128)(2,1)} %maximum_select_fusion.13), channel_id=1, source_target_pairs={{0,8},{1,9},{2,10},{3,11},{4,12},{5,13},{6,14},{7,15},{8,0},{9,1},... | collective-permute-start | bytes 884744 | tf_op jit(solution)/shard_map/ppermute | solution.py:136
  413.1 16.4 %collective-permute-start.8 = (bf16[4,96,768]{2,1,0:T(8,128)(2,1)S(1)}, bf16[4,96,768]{2,1,0:T(8,128)(2,1)S(1)}, u32[]{:S(2)}, u32[]{:S(2)}) collective-permute-start(bf16[4,96,768]{2,1,0:T(8,128)(2,1)S(1)} %dynamic-slice_bitcast_fusion.7), channel_id=1, source_target_pairs={{0,4},{1,5},{2,6},{3,7},{4,0},{5,1},{6,2},{7,3},{8,12},{9,13},{10,... | collective-permute-start | bytes 1769480 | tf_op jit(solution)/shard_map/ppermute | solution.py:136
  414.7 16.9 %collective-permute-start.25 = (bf16[192,768]{1,0:T(8,128)(2,1)S(1)}, bf16[192,768]{1,0:T(8,128)(2,1)S(1)}, u32[]{:S(2)}, u32[]{:S(2)}) collective-permute-start(bf16[192,768]{1,0:T(8,128)(2,1)S(1)} %get-tuple-element.227), channel_id=1, source_target_pairs={{0,2},{1,3},{2,0},{3,1},{4,6},{5,7},{6,4},{7,5},{8,10},{9,11},{10,... | collective-permute-start | bytes 884744 | tf_op jit(solution)/shard_map/ppermute | solution.py:136
  415.6 19.0 %collective-permute-start.27 = (bf16[192,768]{1,0:T(8,128)(2,1)S(1)}, bf16[192,768]{1,0:T(8,128)(2,1)S(1)}, u32[]{:S(2)}, u32[]{:S(2)}) collective-permute-start(bf16[192,768]{1,0:T(8,128)(2,1)S(1)} %get-tuple-element.228), channel_id=1, source_target_pairs={{0,4},{1,5},{2,6},{3,7},{4,0},{5,1},{6,2},{7,3},{8,12},{9,13},{10,... | collective-permute-start | bytes 884744 | tf_op jit(solution)/shard_map/ppermute | solution.py:136
  425.8 26.5 %collective-permute-start.43 = (bf16[2,768,768]{2,1,0:T(8,128)(2,1)}, bf16[2,768,768]{2,1,0:T(8,128)(2,1)}, u32[]{:S(2)}, u32[]{:S(2)}) collective-permute-start(bf16[2,768,768]{2,1,0:T(8,128)(2,1)} %pad_maximum_fusion.3), channel_id=1, source_target_pairs={{0,1},{1,0},{2,3},{3,2},{4,5},{5,4},{6,7},{7,6},{8,9},{9,8},{10,11... | collective-permute-start | bytes 7077896 | tf_op jit(solution)/shard_map/ppermute | solution.py:136
  431.8 13.6 %collective-permute-start.26 = (bf16[384,768]{1,0:T(8,128)(2,1)S(1)}, bf16[384,768]{1,0:T(8,128)(2,1)S(1)}, u32[]{:S(2)}, u32[]{:S(2)}) collective-permute-start(bf16[384,768]{1,0:T(8,128)(2,1)S(1)} %maximum_select_fusion.7), channel_id=1, source_target_pairs={{0,4},{1,5},{2,6},{3,7},{4,0},{5,1},{6,2},{7,3},{8,12},{9,13},{10,... | collective-permute-start | bytes 1769480 | tf_op jit(solution)/shard_map/ppermute | solution.py:136
  448.1 12.5 %collective-permute-start.29 = (bf16[2,768,768]{2,1,0:T(8,128)(2,1)}, bf16[2,768,768]{2,1,0:T(8,128)(2,1)}, u32[]{:S(2)}, u32[]{:S(2)}) collective-permute-start(bf16[2,768,768]{2,1,0:T(8,128)(2,1)} %pad_maximum_fusion.2), channel_id=1, source_target_pairs={{0,1},{1,0},{2,3},{3,2},{4,5},{5,4},{6,7},{7,6},{8,9},{9,8},{10,11... | collective-permute-start | bytes 7077896 | tf_op jit(solution)/shard_map/ppermute | solution.py:136
  (81 other events, 738.0 us)
